TPU v7x, 128 devices: a whole 4x4x4 slice. The times are simulated.
128 devices in a mesh: dp: 16 (over y, z_hi, core), space: 8 (over x, z_lo).
Axes of the slice: x: 4, y: 4, z: 4 (z_hi: 2, z_lo: 2; z = z_hi * 2 + z_lo), core: 2. Of those that a mesh axis runs over, the one named last changes fastest.
Arguments:
- inputs: bfloat16 [128, 32, 32, 1024], P('dp', None, 'space'), may hold values from 0 to 2
- conv_in: bfloat16 [64, 864], replicated, may hold values from -0.21875 to 0.21875
- norm_gain: float32 [64], replicated, may hold values from 0.5 to 1.5
- norm_shift: float32 [64], replicated, may hold values from -3 to 3
- conv_out: bfloat16 [128, 1728], replicated, may hold values from -0.15625 to 0.15625
- dense_in: bfloat16 [65536, 128], replicated, may hold values from -0.0234375 to 0.0234375
- dense_out: bfloat16 [128, 4], replicated, may hold values from -0.5 to 0.5
- targets: float32 [128, 4], P(('dp', 'space')), may hold values from -6 to 6
Outputs:
- grad_conv_in: float32 [64, 864], replicated
- grad_norm: float32 [2, 64], replicated
- grad_conv_out: float32 [128, 1728], replicated
- grad_dense_in: float32 [65536, 128], P(('dp', 'space'))
- grad_dense_out: float32 [128, 4], replicated
- predictions: float32 [128, 4], P(('dp', 'space'))
All inputs are finite; a program needn't handle non-finite values.
Results may differ from a plain program's by a relative error of at most 0.015.
Values may be sent and summed in bfloat16 or wider, within the bound.
A program may use at most 256 MiB of HBM per device.

v0:
```python
import jax
import jax.numpy as jnp
from jax import lax
from jax.sharding import PartitionSpec as P

C_OUT = 128
GRID = 32
norm_epsilon = 1e-05


def extended_2(cells, sides, width):
    for axis, dim in sides:
        count = lax.axis_size(axis)
        ends = count - 1
        head = lax.slice_in_dim(cells, 0, width, axis=dim)
        tail = lax.slice_in_dim(cells, cells.shape[dim] - width, cells.shape[dim], axis=dim)
        cells = jnp.concatenate(
            [
                lax.ppermute(tail, axis, [(i, (i + 1) % count) for i in range(ends)]),
                cells,
                lax.ppermute(head, axis, [((i + 1) % count, i) for i in range(ends)]),
            ],
            axis=dim,
        )
    return cells


def leaky_relu(values):
    return 0.65 * values + 0.35 * values * jnp.tanh(values)


def slope_of(values):
    bent = jnp.tanh(values)
    return 0.65 + 0.35 * (bent + values * (1.0 - bent * bent))


def plane_shift(volume, step_y, step_z, extent):
    plane_len = extent * extent
    offset = step_y * extent + step_z
    margin = extent + 1
    pad_widths = [(0, 0)] * (volume.ndim - 1) + [(margin, margin)]
    padded = jnp.pad(volume, pad_widths)
    shifted = lax.slice_in_dim(
        padded, margin + offset, margin + offset + plane_len, axis=volume.ndim - 1
    )
    column = lax.broadcasted_iota(jnp.int32, (plane_len,), 0) % extent
    inside = ((column + step_z >= 0) & (column + step_z < extent)).astype(volume.dtype)
    return shifted * inside


def columns(slab_ext, planes, extent):
    pieces = []
    for step_x in (-1, 0, 1):
        plane_set = lax.slice_in_dim(slab_ext, 1 + step_x, 1 + step_x + planes, axis=1)
        for step_y in (-1, 0, 1):
            for step_z in (-1, 0, 1):
                pieces.append(plane_shift(plane_set, step_y, step_z, extent))
    stacked = jnp.stack(pieces, 0)
    return stacked.reshape(len(pieces) * slab_ext.shape[0], planes * extent * extent)


def pad_planes(volume, extent):
    shaped = volume.reshape(volume.shape[0], extent, extent * extent)
    return jnp.pad(shaped, ((0, 0), (1, 1), (0, 0)))


def pool_slab(active, planes, extent):
    samples, channels = (active.shape[0], active.shape[1])
    blocks = active.reshape(samples, channels, planes // 2, 2, extent // 2, 2, extent // 2, 2)
    return (blocks.sum(axis=(3, 5, 7)) * 0.125).reshape(samples, channels, -1)


def unpool_slab(gradient, planes, extent):
    samples, channels = (gradient.shape[0], gradient.shape[1])
    blocks = gradient.reshape(samples, channels, planes // 2, 1, extent // 2, 1, extent // 2, 1)
    wide = jnp.broadcast_to(
        blocks, (samples, channels, planes // 2, 2, extent // 2, 2, extent // 2, 2)
    )
    return wide.reshape(samples, channels, planes * extent * extent) * 0.125


def shards(inputs, conv_in, norm_gain, norm_shift, conv_out, dense_in, dense_out, targets):
    half_grid = GRID // 2
    quarter = GRID // 4
    cell_count = inputs.shape[0] * GRID**3
    extended = extended_2(inputs, (("space", 2),), 1)
    planes = extended.shape[2] - 2

    def first_conv(slab_ext):
        return jnp.dot(conv_in, columns(slab_ext, planes, GRID), preferred_element_type=jnp.float32)

    first_out = lax.map(first_conv, extended)
    local_sum = jnp.sum(first_out, axis=(0, 2))
    average = lax.psum(local_sum, "space") / cell_count
    centred = first_out - average[None, :, None]
    variance = lax.psum(jnp.sum(centred * centred, axis=(0, 2)), "space") / cell_count
    inverse = lax.rsqrt(variance + norm_epsilon)
    whitened = centred * inverse[None, :, None]
    normed = norm_gain[None, :, None] * whitened + norm_shift[None, :, None]
    pooled = pool_slab(leaky_relu(normed), planes, GRID).astype(jnp.bfloat16)
    samples_pooled = lax.all_to_all(pooled, "space", split_axis=0, concat_axis=2, tiled=True)

    def second_conv(volume):
        return jnp.dot(
            conv_out,
            columns(pad_planes(volume, half_grid), half_grid, half_grid),
            preferred_element_type=jnp.float32,
        )

    second_out = lax.map(second_conv, samples_pooled)
    local_samples = second_out.shape[0]
    features = (
        pool_slab(leaky_relu(second_out), half_grid, half_grid)
        .reshape(local_samples, -1)
        .astype(jnp.bfloat16)
    )
    hidden_pre = jnp.dot(features, dense_in, preferred_element_type=jnp.float32)
    hidden = leaky_relu(hidden_pre).astype(jnp.bfloat16)
    predictions = jnp.dot(hidden, dense_out, preferred_element_type=jnp.float32)
    misfit = predictions - targets
    grad_out_local = jnp.dot(hidden.astype(jnp.float32).T, misfit, precision=lax.Precision.HIGHEST)
    back_hidden = (
        jnp.dot(misfit, dense_out.astype(jnp.float32).T, precision=lax.Precision.HIGHEST)
        * slope_of(hidden_pre)
    ).astype(jnp.bfloat16)
    grad_dense_in = lax.psum_scatter(
        lax.dot_general(
            features, back_hidden, (((0,), (0,)), ((), ())), preferred_element_type=jnp.float32
        ),
        ("dp", "space"),
        scatter_dimension=0,
        tiled=True,
    )
    back_features = lax.dot_general(
        back_hidden, dense_in, (((1,), (1,)), ((), ())), preferred_element_type=jnp.float32
    )
    back_features = back_features.reshape(local_samples, C_OUT, quarter**3)
    back_second = (unpool_slab(back_features, half_grid, half_grid) * slope_of(second_out)).astype(
        jnp.bfloat16
    )

    def second_back(running, couple):
        volume, gradient = couple
        padded = pad_planes(volume, half_grid)
        patches = columns(padded, half_grid, half_grid)
        running = running + lax.dot_general(
            gradient, patches, (((1,), (1,)), ((), ())), preferred_element_type=jnp.float32
        )
        patch_grad = lax.dot_general(
            conv_out, gradient, (((0,), (0,)), ((), ())), preferred_element_type=jnp.float32
        )
        _, unfold = jax.vjp(
            lambda whole_pad: columns(whole_pad, half_grid, half_grid), padded.astype(jnp.float32)
        )
        volume_grad = unfold(patch_grad)[0][:, 1:-1, :]
        return (running, volume_grad.reshape(volume.shape).astype(jnp.bfloat16))

    grad_conv_out, back_pooled = lax.scan(
        second_back, jnp.zeros(conv_out.shape, jnp.float32), (samples_pooled, back_second)
    )
    back_slab = lax.all_to_all(back_pooled, "space", split_axis=2, concat_axis=0, tiled=True)
    back_active = unpool_slab(back_slab.astype(jnp.float32), planes, GRID) * slope_of(normed)
    sum_grad = jnp.sum(back_active, axis=(0, 2))
    sum_xgrad = jnp.sum(back_active * whitened, axis=(0, 2))
    group_grad, group_xgrad = lax.psum((sum_grad, sum_xgrad), "space")
    back_first = (norm_gain * inverse)[None, :, None] * (
        back_active
        - group_grad[None, :, None] / cell_count
        - whitened * group_xgrad[None, :, None] / cell_count
    )
    back_first = back_first.astype(jnp.bfloat16)

    def first_back(running, couple):
        slab_ext, gradient = couple
        patches = columns(slab_ext, planes, GRID)
        return (
            running
            + lax.dot_general(
                gradient, patches, (((1,), (1,)), ((), ())), preferred_element_type=jnp.float32
            ),
            None,
        )

    grad_conv_in, _ = lax.scan(
        first_back, jnp.zeros(conv_in.shape, jnp.float32), (extended, back_first)
    )
    grad_norm_local = jnp.stack([sum_xgrad, sum_grad])
    summed = lax.psum(
        (grad_conv_in, grad_norm_local, grad_conv_out, grad_out_local), ("dp", "space")
    )
    return (summed[0], summed[1], summed[2], grad_dense_in, summed[3], predictions)


def solution(mesh):
    placed = (P("dp", None, "space", None), P(), P(), P(), P(), P(), P(), P(("dp", "space"), None))
    return jax.shard_map(
        shards,
        mesh=mesh,
        in_specs=placed,
        out_specs=(P(), P(), P(), P(("dp", "space"), None), P(), P(("dp", "space"), None)),
        check_vma=False,
    )
```

profile of v0, /device:TPU:0, one launch (start us, length us, event | category | flops | bytes accessed | tf_op | source)
XLA Modules:
  0.0 1617.1 jit_solution(11225034496510748048)
XLA Ops:
  7.2 4.1 fusion.158
  13.8 5.3 collective-permute-start
  19.1 8.3 collective-permute-done.1
  29.4 9.5 collective-permute-done
  40.7 4.8 pad_maximum_fusion
  45.6 131.2 %while.34 = (s32[]{:T(128)}, f32[8,64,4096]{2,1,0:T(8,128)}, bf16[8,32,6,1024]{3,2,1,0:T(8,128)(2,1)}, bf16[64,864]{1,0:T(8,128)(2,1)}, s32[]{:T(128)}) while((s32[]{:T(128)}, f32[8,64,4096]{2,1,0:T(8,128)}, bf16[8,32,6,1024]{3,2,1,0:T(8,128)(2,1)}, bf16[64,864]{1,0:T(8,128)(2,1)}, s32[]{:T(128)}) %tuple.124), condition=%wide.region_1.2_spmd, body=%wide.region_0.1_spmd.sunk | while | flops 467173376 | bytes 38973516 | solution.py:92
  54.2 4.6 copy.86
  58.8 3.3 fusion.194
  70.5 4.6 copy.86
  86.8 4.6 copy.86
  103.1 4.6 copy.86
  119.4 4.6 copy.86
  124.0 3.3 fusion.194
  135.7 4.6 copy.86
  140.4 3.3 fusion.194
  152.0 4.6 copy.86
  168.3 4.6 copy.86
  172.9 3.4 fusion.194
  176.8 12.3 copy.39
  189.1 4.0 reduce_sum.54
  193.1 19.2 %psum.56 = f32[64]{0:T(128)S(1)} all-reduce(f32[64]{0:T(128)S(1)} %reduce_sum.54), channel_id=1, replica_groups=mesh['dp'=16,'space'=8] {'space'}, use_global_device_ids=true, to_apply=%region_3.4 | all-reduce | flops 64 | bytes 512 | tf_op jit(solution)/shard_map/psum | solution.py:94
  212.3 8.1 multiply_reduce_fusion.1
  220.4 16.4 %psum.57 = f32[64]{0:T(128)S(1)} all-reduce(f32[64]{0:T(128)S(1)} %multiply_reduce_fusion.1), channel_id=1, replica_groups=mesh['dp'=16,'space'=8] {'space'}, use_global_device_ids=true, to_apply=%region_5.6 | all-reduce | flops 64 | bytes 512 | tf_op jit(solution)/shard_map/psum | solution.py:96
  236.8 12.9 fusion.38
  249.8 7.7 reduce_sum.56
  261.4 3.5 all-to-all-start
  265.0 8.0 all-to-all-done
  280.1 5.6 copy.56
  285.7 5.7 fusion.40
  298.0 7.5 convert_convert_fusion
  306.3 78.6 %fusion.140 = f32[1,128,8,8,8]{4,0,3,2,1:T(1,128)} fusion(bf16[128,8,8,8,128]{4,3,2,1,0:T(8,128)(2,1)} %bitcast.529, bf16[128]{0:T(256)(128)(2,1)S(1)} %get-tuple-element.270), kind=kOutput, calls=%fused_computation.309 | convolution fusion | flops 16777216 | bytes 17039616 | tf_op jit(solution)/shard_map/dot_general | solution.py:134
  384.9 8.7 copy.49
  397.7 11.3 convolution_bitcast_fusion.1
  409.0 6.2 fusion.157
  415.2 11.4 fusion.156
  454.1 5.9 bitcast_multiply_fusion.19
  460.0 5.9 bitcast_multiply_fusion.21
  465.9 7.5 fusion.50
  473.5 8.7 fusion.58
  483.6 5.3 copy.45
  489.5 24.4 %reduce.1 = bf16[4096,64]{1,0:T(8,128)(2,1)} reduce(bf16[4096,1,64]{2,1,0:T(2,128)(2,1)} %bitcast.534, bf16[]{:T(256)} %broadcast.801), dimensions={1}, to_apply=%bitcast.376.reduce_sub_computation | reduce | bytes 1048578
  517.1 3.5 all-to-all-start.1
  520.6 10.0 fusion.160
  538.2 11.5 fusion.39
  549.7 20.0 %all-reduce.39 = (f32[64]{0:T(128)S(1)}, f32[64]{0:T(128)S(1)}) all-reduce(f32[64]{0:T(128)S(1)} %get-tuple-element.176, f32[64]{0:T(128)S(1)} %get-tuple-element.175), channel_id=1, replica_groups=mesh['dp'=16,'space'=8] {'space'}, use_global_device_ids=true, to_apply=%region_11.12 | all-reduce | flops 128 | bytes 1024 | tf_op jit(solution)/shard_map/psum | solution.py:165
  569.6 14.0 multiply_convert_fusion
  583.7 9.8 copy.47
  593.4 136.7 %while.35 = (s32[]{:T(128)}, f32[64,864]{1,0:T(8,128)}, bf16[8,64,4096]{2,1,0:T(8,128)(2,1)}, bf16[8,32,6,1024]{3,2,1,0:T(8,128)(2,1)}, s32[]{:T(128)}, /*index=5*/s32[]{:T(128)}) while((s32[]{:T(128)}, f32[64,864]{1,0:T(8,128)}, bf16[8,64,4096]{2,1,0:T(8,128)(2,1)}, bf16[8,32,6,1024]{3,2,1,0:T(8,128)(2,1)}, s32[]{:T(128)}, ...), condition=%wide.region_13.14_spmd.clone, body=%wide.region_12.13_spmd.clone.sunk | while | flops 467283968 | bytes 40546452 | solution.py:184
  602.0 4.6 copy.87
  619.0 4.6 copy.87
  636.1 4.6 copy.87
  640.7 3.3 convolution_add_fusion.2
  653.1 4.6 copy.87
  657.7 3.3 convolution_add_fusion.2
  670.1 4.6 copy.87
  687.1 4.6 copy.87
  691.8 3.3 convolution_add_fusion.2
  704.2 4.6 copy.87
  708.8 3.3 convolution_add_fusion.2
  721.2 4.6 copy.87
  730.2 25.5 %broadcast_multiply_fusion = f32[65536,128]{1,0:T(8,128)} fusion(f32[128]{0:T(128)S(1)} %copy-done.25, f32[65536]{0:T(1024)} %convert.13), kind=kLoop, calls=%fused_computation.102 | loop fusion | flops 8388608 | bytes 33817088 | tf_op jit(solution)/shard_map/dot_general | solution.py:127
  756.5 64.4 %all-reduce.37 = (f32[2,64]{1,0:T(2,128)}, f32[128,4]{0,1:T(4,128)}) all-reduce(f32[2,64]{1,0:T(2,128)S(1)} %pad_maximum_fusion.1, f32[128,4]{0,1:T(4,128)S(1)} %broadcast_multiply_fusion.1), channel_id=1, replica_groups=mesh['dp'=16,'space'=8] {'dp','space'}, use_global_device_ids=true, to_apply=%region_15.16 | all-reduce | flops 640 | bytes 5120 | tf_op jit(solution)/shard_map/psum | solution.py:188
  820.8 56.8 %all-reduce.42.cloned.1.call-done = (f32[64,864]{1,0:T(8,128)}, f32[128,1728]{0,1:T(8,128)}) async-done(((f32[64,864]{1,0:T(8,128)}, f32[128,1728]{0,1:T(8,128)}), (f32[64,864]{1,0:T(8,128)}, f32[128,1728]{0,1:T(8,128)})) %all-reduce.42.cloned.1.call-update) | async-done | bytes 1105936 | tf_op jit(solution)/shard_map/psum | solution.py:188
  877.7 728.4 %reduce-scatter.2.cloned.1.call-done = f32[512,128]{1,0:T(8,128)} async-done(((f32[65536,128]{1,0:T(8,128)}), f32[512,128]{1,0:T(8,128)}) %reduce-scatter.2.cloned.1.call-update) | async-done | bytes 262160 | tf_op jit(solution)/shard_map/reduce_scatter | solution.py:126
  (715 shorter events, 238.0 us)
Async XLA Ops:
  7.2 278.6 %copy-start = (bf16[128,1728]{0,1:T(8,128)(2,1)S(1)}, bf16[128,1728]{0,1:T(8,128)(2,1)}, u32[]{:S(2)}) copy-start(bf16[128,1728]{0,1:T(8,128)(2,1)} %param.16) | copy-start | bytes 1327108
  7.2 33.6 %copy-start.3 = (bf16[8,32,4,1024]{3,2,1,0:T(4,128)(2,1)S(1)}, bf16[8,32,4,1024]{3,2,1,0:T(4,128)(2,1)}, u32[]{:S(2)}) copy-start(bf16[8,32,4,1024]{3,2,1,0:T(4,128)(2,1)} %param.12) | copy-start | bytes 6291460
  11.5 15.9 collective-permute-start.1
  13.8 25.1 %collective-permute-start = (bf16[8,32,1,1024]{3,1,2,0:T(8,128)(2,1)}, bf16[8,32,1,1024]{3,1,2,0:T(8,128)(2,1)}, u32[]{:S(2)}, u32[]{:S(2)}) collective-permute-start(bf16[8,32,1,1024]{3,1,2,0:T(8,128)(2,1)} %copy.52), channel_id=1, source_target_pairs={{0,1},{1,2},{2,3},{3,4},{4,5},{5,6},{6,7},{8,9},{9,10},{10,11},{11... | collective-permute-start | bytes 1572872 | tf_op jit(solution)/shard_map/ppermute | solution.py:19
  212.3 24.5 %copy-start.22 = (f32[64]{0:T(128)S(1)}, f32[64]{0:T(128)}, u32[]{:S(2)}) copy-start(f32[64]{0:T(128)} %param.14) | copy-start | bytes 772
  212.3 24.5 %copy-start.23 = (f32[64]{0:T(128)S(1)}, f32[64]{0:T(128)}, u32[]{:S(2)}) copy-start(f32[64]{0:T(128)} %param.15) | copy-start | bytes 772
  261.4 11.6 all-to-all-start
  285.7 5.7 copy-start.2
  298.0 7.5 copy-start.26
  298.0 7.6 copy-start.27
  305.6 79.2 %copy-start.29 = (f32[1,4]{1,0:T(1,128)}, f32[1,4]{1,0:T(1,128)S(1)}, u32[]{:S(2)}) copy-start(f32[1,4]{1,0:T(1,128)S(1)} %fusion.150) | copy-start | bytes 52
  396.7 1.0 copy-start.6
  426.6 5.3 copy-start.21
  426.6 5.7 copy-start.20
  426.6 6.0 copy-start.19
  427.9 6.0 copy-start.17
  429.6 4.7 copy-start.15
  431.2 3.4 copy-start.18
  431.6 4.4 copy-start.16
  431.9 4.3 copy-start.14
  432.6 6.3 copy-start.13
  433.9 5.2 copy-start.12
  434.6 7.2 copy-start.11
  435.9 6.2 copy-start.10
  436.3 7.2 copy-start.9
  437.6 7.2 copy-start.8
  438.8 7.2 copy-start.7
  517.1 16.4 %all-to-all-start.1 = ((bf16[8,2,16384]{2,1,0:T(2,128)(2,1)}), bf16[8,2,16384]{2,1,0:T(2,128)(2,1)S(1)}, u32[]{:S(2)}, u32[]{:S(2)}) async-start(bf16[8,2,16384]{2,1,0:T(2,128)(2,1)} %reshape.342), calls=%async_computation.1 | async-start | bytes 1048576 | tf_op jit(solution)/shard_map/all_to_all | solution.py:161
  520.6 357.1 %all-reduce.42.cloned.1.call-start = ((), (), s32[]{:S(2)}) async-start(), calls=%async_computation.4 | async-start | bytes 2228224 | tf_op jit(solution)/shard_map/psum | solution.py:188
  593.4 136.7 %copy-start.25 = (f32[128]{0:T(128)S(1)}, f32[128]{0:T(128)}, u32[]{:S(2)}) copy-start(f32[128]{0:T(128)} %get-tuple-element.269) | copy-start | bytes 1540
  602.0 4.7 copy-start.4
  610.0 0.7 copy-start.5
  619.0 4.7 copy-start.4
  627.0 0.7 copy-start.5
  636.0 4.7 copy-start.4
  644.0 0.7 copy-start.5
  653.1 4.7 copy-start.4
  661.0 0.7 copy-start.5
  670.1 4.7 copy-start.4
  678.1 0.7 copy-start.5
  687.1 4.7 copy-start.4
  695.1 0.7 copy-start.5
  704.2 4.7 copy-start.4
  712.1 0.7 copy-start.5
  721.2 4.7 copy-start.4
  729.1 0.7 copy-start.5
  730.1 875.9 %reduce-scatter.2.cloned.1.call-start = ((), (), s32[]{:S(2)}) async-start(), calls=%async_computation.3 | async-start | bytes 33816576 | tf_op jit(solution)/shard_map/reduce_scatter | solution.py:126
  755.7 0.7 copy-start.28
  755.7 0.7 copy-start.30
  755.7 0.7 copy-start.24
  756.4 853.4 %copy-start.1 = (bf16[128,1728]{0,1:T(8,128)(2,1)S(1)}, bf16[128,1728]{0,1:T(8,128)(2,1)}, u32[]{:S(2)}) copy-start(bf16[128,1728]{0,1:T(8,128)(2,1)} %param.16) | copy-start | bytes 1327108
Sparse Core Ops, SparseCore 0:
  730.2 147.3 all-reduce.41
  880.8 725.2 reduce-scatter.1
where the time goes:
time: 1620 us
  waiting for transfers between devices  811 us (50%)
  other arithmetic  267 us (16%)
  local copies, waits for them, and re-layouts  221 us (14%)
  matrix products  167 us (10%)
  blocking collectives  120 us (7%)
    reduce_scatter x1, waiting for transfers between devices, shards(): lax.psum_scatter(lax.dot_general(features, back_hidden, (((0,), (0,)), ((...  728 us
    while x416, other arithmetic  107 us
    while x48, local copies, waits for them, and re-layouts  79.7 us
    dot_general x1, matrix products, shards(): lax.dot_general(back_hidden, dense_in, (((1,), (1,)), ((), ())), preferre...  78.6 us
    psum x1, blocking collectives, shards(): lax.psum((grad_conv_in, grad_norm_local, grad_conv_out, grad_out_local),...  64.4 us
    psum x1, waiting for transfers between devices, shards(): lax.psum((grad_conv_in, grad_norm_local, grad_conv_out, grad_out_local),...  56.8 us
    unnamed x94, local copies, waits for them, and re-layouts  53.9 us
  transfers between devices with their start and end apart: 6, of which 5 were waited for; matrix products, arithmetic and copies ran while one was open for 3% of the time, Pallas kernels for 0%

commit v1 on v0

--- a/solution.py
+++ b/solution.py
@@ -1,3 +1,4 @@
+import functools
 import jax
 import jax.numpy as jnp
 from jax import lax
@@ -6,6 +7,14 @@
 C_OUT = 128
 GRID = 32
 norm_epsilon = 1e-05
+
+
+def detail_the_frame(page, link_axis, net_axis):
+    before = lax.psum(page, link_axis)
+    return lax.psum(before, net_axis)
+
+
+move_columns = functools.partial(detail_the_frame, link_axis="space", net_axis="dp")
 
 
 def extended_2(cells, sides, width):
@@ -185,9 +194,7 @@
         first_back, jnp.zeros(conv_in.shape, jnp.float32), (extended, back_first)
     )
     grad_norm_local = jnp.stack([sum_xgrad, sum_grad])
-    summed = lax.psum(
-        (grad_conv_in, grad_norm_local, grad_conv_out, grad_out_local), ("dp", "space")
-    )
+    summed = move_columns((grad_conv_in, grad_norm_local, grad_conv_out, grad_out_local))
     return (summed[0], summed[1], summed[2], grad_dense_in, summed[3], predictions)
 
 

time: 1620 us -> 1590 us (0.981)
  blocking collectives: 120 us -> 90.2 us
    reduce_scatter x1, waiting for transfers between devices: 728 us -> 558 us  [shards(): lax.psum_scatter(lax.dot_general(features, back_hidden, (((0,), (0,)), ((...]
    psum x1 -> x2, waiting for transfers between devices: 56.8 us -> 223 us  [the longest x1 148 us: detail_the_frame(): return lax.psum(before, net_axis)]
    psum x1, blocking collectives: 64.4 us -> 34.6 us  [detail_the_frame(): return lax.psum(before, net_axis)]
  transfers between devices with their start and end apart: 6 -> 7, of which waited for: 5 -> 6; matrix products, arithmetic and copies ran while one was open for 3% -> 3% of each run, Pallas kernels for 0% -> 0%
where the time goes in v1:
time: 1590 us; the launch traced here: 1570 us
  waiting for transfers between devices  807 us (51%)
  other arithmetic  264 us (17%)
  local copies, waits for them, and re-layouts  215 us (14%)
  matrix products  166 us (10%)
  blocking collectives  90.2 us (6%)
  between operations  16.6 us (1%)
    reduce_scatter x1, waiting for transfers between devices, shards(): lax.psum_scatter(lax.dot_general(features, back_hidden, (((0,), (0,)), ((...  558 us
    psum x1, waiting for transfers between devices, detail_the_frame(): return lax.psum(before, net_axis)  148 us
    while x416, other arithmetic  107 us
    while x48, local copies, waits for them, and re-layouts  79.7 us
    dot_general x1, matrix products, shards(): lax.dot_general(back_hidden, dense_in, (((1,), (1,)), ((), ())), preferre...  78.3 us
    psum x1, waiting for transfers between devices, detail_the_frame(): before = lax.psum(page, link_axis)  74.8 us
    unnamed x94, local copies, waits for them, and re-layouts  49.2 us
    psum x1, blocking collectives, detail_the_frame(): return lax.psum(before, net_axis)  34.6 us
  transfers between devices with their start and end apart: 7, of which 6 were waited for; matrix products, arithmetic and copies ran while one was open for 3% of the time, Pallas kernels for 0%

profile of v1, /device:TPU:0, one launch (start us, length us, event | category | flops | bytes accessed | tf_op | source)
XLA Modules:
  0.0 1574.8 jit_solution(11948206350887267564)
XLA Ops:
  8.0 4.1 fusion.158
  14.6 5.3 collective-permute-start
  19.9 8.3 collective-permute-done.1
  30.2 9.5 collective-permute-done
  41.6 4.9 pad_maximum_fusion
  46.4 131.2 %while.34 = (s32[]{:T(128)}, f32[8,64,4096]{2,1,0:T(8,128)}, bf16[8,32,6,1024]{3,2,1,0:T(8,128)(2,1)}, bf16[64,864]{1,0:T(8,128)(2,1)}, s32[]{:T(128)}) while((s32[]{:T(128)}, f32[8,64,4096]{2,1,0:T(8,128)}, bf16[8,32,6,1024]{3,2,1,0:T(8,128)(2,1)}, bf16[64,864]{1,0:T(8,128)(2,1)}, s32[]{:T(128)}) %tuple.124), condition=%wide.region_1.2_spmd, body=%wide.region_0.1_spmd.sunk | while | flops 467173376 | bytes 38973516 | solution.py:101
  55.3 4.6 copy.86
  60.0 3.3 fusion.194
  71.7 4.6 copy.86
  87.9 4.6 copy.86
  92.6 3.3 fusion.194
  104.3 4.6 copy.86
  120.5 4.6 copy.86
  125.2 3.3 fusion.194
  136.9 4.6 copy.86
  153.2 4.6 copy.86
  169.4 4.6 copy.86
  174.1 3.4 fusion.194
  177.6 12.3 copy.39
  189.9 4.0 reduce_sum.54
  193.9 19.2 %psum.84 = f32[64]{0:T(128)S(1)} all-reduce(f32[64]{0:T(128)S(1)} %reduce_sum.54), channel_id=1, replica_groups=mesh['dp'=16,'space'=8] {'space'}, use_global_device_ids=true, to_apply=%region_3.4 | all-reduce | flops 64 | bytes 512 | tf_op jit(solution)/shard_map/psum | solution.py:103
  213.1 8.1 multiply_reduce_fusion.1
  221.2 16.4 %psum.85 = f32[64]{0:T(128)S(1)} all-reduce(f32[64]{0:T(128)S(1)} %multiply_reduce_fusion.1), channel_id=1, replica_groups=mesh['dp'=16,'space'=8] {'space'}, use_global_device_ids=true, to_apply=%region_5.6 | all-reduce | flops 64 | bytes 512 | tf_op jit(solution)/shard_map/psum | solution.py:105
  237.7 12.9 fusion.38
  250.6 7.7 reduce_sum.56
  262.3 3.5 all-to-all-start
  265.8 8.0 all-to-all-done
  281.0 5.8 copy.56
  286.8 5.7 fusion.40
  299.1 7.0 convert_convert_fusion
  306.9 78.3 %fusion.140 = f32[1,128,8,8,8]{4,0,3,2,1:T(1,128)} fusion(bf16[128,8,8,8,128]{4,3,2,1,0:T(8,128)(2,1)} %bitcast.529, bf16[128]{0:T(256)(128)(2,1)S(1)} %get-tuple-element.274), kind=kOutput, calls=%fused_computation.309 | convolution fusion | flops 16777216 | bytes 17039616 | tf_op jit(solution)/shard_map/dot_general | solution.py:143
  385.3 8.9 copy.49
  396.6 11.2 convolution_bitcast_fusion.1
  407.9 5.9 fusion.157
  413.7 11.7 fusion.156
  448.5 5.5 bitcast_multiply_fusion.19
  454.0 4.9 bitcast_multiply_fusion.21
  459.0 6.6 fusion.50
  465.6 8.7 fusion.58
  478.3 23.4 %reduce.1 = bf16[4096,64]{1,0:T(8,128)(2,1)} reduce(bf16[4096,1,64]{2,1,0:T(2,128)(2,1)S(1)} %bitcast.534, bf16[]{:T(256)} %broadcast.801), dimensions={1}, to_apply=%bitcast.376.reduce_sub_computation | reduce | bytes 1048578
  501.7 3.4 reshape.342
  505.1 3.5 all-to-all-start.1
  508.6 10.0 fusion.160
  523.4 11.5 fusion.39
  534.9 20.0 %all-reduce.39 = (f32[64]{0:T(128)S(1)}, f32[64]{0:T(128)S(1)}, f32[2,64]{1,0:T(2,128)S(1)}, f32[128,4]{0,1:T(4,128)S(1)}) all-reduce(f32[64]{0:T(128)S(1)} %get-tuple-element.176, f32[64]{0:T(128)S(1)} %get-tuple-element.175, f32[2,64]{1,0:T(2,128)S(1)} %pad_maximum_fusion.1, ...), channel_id=1, replica_groups=mesh['dp'=16,'space'=8] {'space'}, use_global_device_ids=true, to_apply=%region_11.12 | all-reduce | flops 768 | bytes 6144 | tf_op jit(solution)/shard_map/psum | solution.py:174
  554.9 14.0 multiply_convert_fusion
  568.9 9.8 copy.47
  578.7 136.6 %while.35 = (s32[]{:T(128)}, f32[64,864]{1,0:T(8,128)}, bf16[8,64,4096]{2,1,0:T(8,128)(2,1)}, bf16[8,32,6,1024]{3,2,1,0:T(8,128)(2,1)}, s32[]{:T(128)}, /*index=5*/s32[]{:T(128)}) while((s32[]{:T(128)}, f32[64,864]{1,0:T(8,128)}, bf16[8,64,4096]{2,1,0:T(8,128)(2,1)}, bf16[8,32,6,1024]{3,2,1,0:T(8,128)(2,1)}, s32[]{:T(128)}, ...), condition=%wide.region_13.14_spmd.clone, body=%wide.region_12.13_spmd.clone.sunk | while | flops 467283968 | bytes 40546452 | solution.py:193
  587.3 4.6 copy.87
  604.3 4.6 copy.87
  621.3 4.6 copy.87
  626.0 3.3 convolution_add_fusion.2
  638.3 4.6 copy.87
  655.4 4.6 copy.87
  672.4 4.6 copy.87
  689.4 4.6 copy.87
  706.4 4.6 copy.87
  711.1 3.3 convolution_add_fusion.2
  715.4 3.5 convert_element_type.610
  718.9 74.8 %all-reduce.46.cloned.1.call-done = (f32[64,864]{1,0:T(8,128)}, f32[128,1728]{0,1:T(8,128)}) async-done(((f32[64,864]{1,0:T(8,128)}, f32[128,1728]{0,1:T(8,128)}), (f32[64,864]{1,0:T(8,128)}, f32[128,1728]{0,1:T(8,128)})) %all-reduce.46.cloned.1.call-update) | async-done | bytes 1105936 | tf_op jit(solution)/shard_map/psum | solution.py:13
  793.8 28.7 %broadcast_multiply_fusion = f32[65536,128]{1,0:T(8,128)} fusion(f32[128]{0:T(128)S(1)} %copy-done.27, f32[65536]{0:T(1024)S(1)} %convert.13), kind=kLoop, calls=%fused_computation.102 | loop fusion | flops 8388608 | bytes 33817088 | tf_op jit(solution)/shard_map/dot_general | solution.py:136
  822.6 34.6 %all-reduce.37 = (f32[2,64]{1,0:T(2,128)}, f32[128,4]{0,1:T(4,128)}) all-reduce(f32[2,64]{1,0:T(2,128)S(1)} %get-tuple-element.199, f32[128,4]{0,1:T(4,128)S(1)} %get-tuple-element.200), channel_id=1, replica_groups=mesh['dp'=16,'space'=8] {'dp'}, use_global_device_ids=true, to_apply=%region_17.18 | all-reduce | flops 640 | bytes 5120 | tf_op jit(solution)/shard_map/psum | solution.py:14
  857.2 147.9 %all-reduce.44.cloned.1.call-done = (f32[64,864]{1,0:T(8,128)}, f32[128,1728]{0,1:T(8,128)}) async-done(((f32[64,864]{1,0:T(8,128)}, f32[128,1728]{0,1:T(8,128)}), (f32[64,864]{1,0:T(8,128)}, f32[128,1728]{0,1:T(8,128)})) %all-reduce.44.cloned.1.call-update) | async-done | bytes 1105936 | tf_op jit(solution)/shard_map/psum | solution.py:14
  1005.1 558.2 %reduce-scatter.2.cloned.1.call-done = f32[512,128]{1,0:T(8,128)} async-done(((f32[65536,128]{1,0:T(8,128)}), f32[512,128]{1,0:T(8,128)}) %reduce-scatter.2.cloned.1.call-update) | async-done | bytes 262160 | tf_op jit(solution)/shard_map/reduce_scatter | solution.py:135
  (718 shorter events, 233.8 us)
Async XLA Ops:
  8.0 278.8 %copy-start = (bf16[128,1728]{0,1:T(8,128)(2,1)S(1)}, bf16[128,1728]{0,1:T(8,128)(2,1)}, u32[]{:S(2)}) copy-start(bf16[128,1728]{0,1:T(8,128)(2,1)} %param.16) | copy-start | bytes 1327108
  8.0 33.6 %copy-start.4 = (bf16[8,32,4,1024]{3,2,1,0:T(4,128)(2,1)S(1)}, bf16[8,32,4,1024]{3,2,1,0:T(4,128)(2,1)}, u32[]{:S(2)}) copy-start(bf16[8,32,4,1024]{3,2,1,0:T(4,128)(2,1)} %param.12) | copy-start | bytes 6291460
  12.3 15.9 %collective-permute-start.1 = (bf16[8,32,1,1024]{3,1,2,0:T(8,128)(2,1)S(1)}, bf16[8,32,1,1024]{3,1,2,0:T(8,128)(2,1)}, u32[]{:S(2)}, u32[]{:S(2)}) collective-permute-start(bf16[8,32,1,1024]{3,1,2,0:T(8,128)(2,1)S(1)} %copy.53), channel_id=1, source_target_pairs={{1,0},{2,1},{3,2},{4,3},{5,4},{6,5},{7,6},{9,8},{10,9},{11,10},{12... | collective-permute-start | bytes 1572872 | tf_op jit(solution)/shard_map/ppermute | solution.py:30
  14.6 25.1 %collective-permute-start = (bf16[8,32,1,1024]{3,1,2,0:T(8,128)(2,1)}, bf16[8,32,1,1024]{3,1,2,0:T(8,128)(2,1)}, u32[]{:S(2)}, u32[]{:S(2)}) collective-permute-start(bf16[8,32,1,1024]{3,1,2,0:T(8,128)(2,1)} %copy.52), channel_id=1, source_target_pairs={{0,1},{1,2},{2,3},{3,4},{4,5},{5,6},{6,7},{8,9},{9,10},{10,11},{11... | collective-permute-start | bytes 1572872 | tf_op jit(solution)/shard_map/ppermute | solution.py:28
  213.1 24.5 %copy-start.25 = (f32[64]{0:T(128)S(1)}, f32[64]{0:T(128)}, u32[]{:S(2)}) copy-start(f32[64]{0:T(128)} %param.14) | copy-start | bytes 772
  213.1 24.5 %copy-start.26 = (f32[64]{0:T(128)S(1)}, f32[64]{0:T(128)}, u32[]{:S(2)}) copy-start(f32[64]{0:T(128)} %param.15) | copy-start | bytes 772
  262.3 11.6 all-to-all-start
  286.8 5.7 copy-start.3
  296.8 9.3 copy-start.2
  299.1 7.0 copy-start.28
  299.1 7.1 copy-start.29
  306.3 212.4 %copy-start.30 = (f32[1,4]{1,0:T(1,128)}, f32[1,4]{1,0:T(1,128)S(1)}, u32[]{:S(2)}) copy-start(f32[1,4]{1,0:T(1,128)S(1)} %fusion.150) | copy-start | bytes 52
  385.2 9.7 copy-start.24
  395.7 1.0 copy-start.7
  425.5 1.7 copy-start.23
  425.5 2.4 copy-start.22
  425.8 2.4 copy-start.20
  426.1 2.4 copy-start.18
  426.5 2.4 copy-start.21
  426.8 3.4 copy-start.19
  427.2 3.4 copy-start.17
  427.5 4.4 copy-start.16
  427.8 5.3 copy-start.15
  428.2 5.3 copy-start.14
  428.9 7.2 copy-start.13
  430.2 6.2 copy-start.12
  430.5 7.2 copy-start.11
  431.9 7.2 copy-start.10
  433.2 7.2 copy-start.9
  448.5 5.5 copy-start.8
  505.1 13.6 all-to-all-start.1
  508.6 285.1 %all-reduce.46.cloned.1.call-start = ((), (), s32[]{:S(2)}) async-start(), calls=%async_computation.5 | async-start | bytes 2228224 | tf_op jit(solution)/shard_map/psum | solution.py:13
  578.7 215.1 %copy-start.27 = (f32[128]{0:T(128)S(1)}, f32[128]{0:T(128)}, u32[]{:S(2)}) copy-start(f32[128]{0:T(128)} %get-tuple-element.273) | copy-start | bytes 1540
  587.2 4.7 copy-start.5
  595.2 0.7 copy-start.6
  604.3 4.7 copy-start.5
  612.2 0.7 copy-start.6
  621.3 4.7 copy-start.5
  629.3 0.7 copy-start.6
  638.3 4.7 copy-start.5
  646.3 0.7 copy-start.6
  655.3 4.7 copy-start.5
  663.3 0.7 copy-start.6
  672.4 4.7 copy-start.5
  680.3 0.7 copy-start.6
  689.4 4.7 copy-start.5
  697.4 0.7 copy-start.6
  706.4 4.7 copy-start.5
  714.4 0.7 copy-start.6
  715.3 289.8 %all-reduce.44.cloned.1.call-start = ((), (), s32[]{:S(2)}) async-start(), calls=%async_computation.4 | async-start | bytes 2228224 | tf_op jit(solution)/shard_map/psum | solution.py:14
  793.7 769.6 %reduce-scatter.2.cloned.1.call-start = ((), (), s32[]{:S(2)}) async-start(), calls=%async_computation.3 | async-start | bytes 33816576 | tf_op jit(solution)/shard_map/reduce_scatter | solution.py:135
  822.6 744.6 %copy-start.1 = (bf16[128,1728]{0,1:T(8,128)(2,1)S(1)}, bf16[128,1728]{0,1:T(8,128)(2,1)}, u32[]{:S(2)}) copy-start(bf16[128,1728]{0,1:T(8,128)(2,1)} %param.16) | copy-start | bytes 1327108
Sparse Core Ops, SparseCore 0:
  715.4 78.2 all-reduce.45
  796.5 208.6 all-reduce.43
Sparse Core Ops, SparseCore 1:
  822.6 740.7 reduce-scatter.1
